TPU v7x, 256 devices: a whole 4x4x8 slice. The times are simulated.
256 devices in a mesh: shot: 8 (over y, core), band: 32 (over x, z).
Axes of the slice: x: 4, y: 4, z: 8, core: 2. Of those that a mesh axis runs over, the one named last changes fastest.
Arguments:
- sensitivity: bfloat16 [16384, 128, 128], P(('shot', 'band')), may hold values from -0.0625 to 0.0625
- bundle_of: int32 [16384], P(('shot', 'band')), may hold values from 0 to 31
- cellblock_of: int32 [16384], P(('shot', 'band')), may hold values from 0 to 15
- state: float32 [65536, 128], P('band'), may hold values from -6 to 6
- prior_velocity: float32 [65536, 128], P('band'), may hold values from -6 to 6
- observed: float32 [256, 128], P(('shot', 'band')), may hold values from -6 to 6
- pick_weight: float32 [256, 128], P(('shot', 'band')), may hold values from 0.3 to 3
Outputs:
- new_state: float32 [65536, 128], P('band')
- weighted_residual: float32 [256, 128, 128], P(('shot', 'band'))
Inputs may be any that keep to these rules, and one draw needn't show every extreme that they name: bundle_of names a bundle of the block's own source group. cellblock_of names a cell block of the block's own depth band.
All inputs are finite; a program needn't handle non-finite values.
Results may differ from a plain program's by a relative error of at most 0.0059.
Values may be sent and summed in bfloat16 or wider, within the bound.
A program may use at most 64 MiB of HBM per device.

v0:
```python
import jax
import jax.numpy as jnp
from jax import lax
from jax.sharding import PartitionSpec as P

CBLK = 128


def block_products(sensitivity, cellblock_of, probe):
    columns = probe.reshape(-1, CBLK, probe.shape[1])[cellblock_of]
    return jnp.einsum("krc,kce->kre", sensitivity, columns, preferred_element_type=jnp.float32)


def adjoint_part(sensitivity, bundle_of, cellblock_of, resid_all, cell_blocks):
    rows = resid_all[bundle_of]
    contrib = jnp.einsum("krc,kre->kce", sensitivity, rows, preferred_element_type=jnp.float32)
    summed = jax.ops.segment_sum(contrib, cellblock_of, num_segments=cell_blocks)
    return summed.reshape(cell_blocks * CBLK, rows.shape[2])


def per_device(sensitivity, bundle_of, cellblock_of, state, prior_velocity, observed, pick_weight):
    nband = lax.axis_size("band")
    owned = observed.shape[0]
    bundles = owned * nband
    cell_blocks = state.shape[0] // CBLK

    def residual_pass(probe):
        prod = block_products(sensitivity, cellblock_of, probe)
        partial_value = jax.ops.segment_sum(prod, bundle_of, num_segments=bundles)
        pred = lax.psum_scatter(partial_value, "band", scatter_dimension=0, tiled=True)
        resid = pick_weight[:, :, None] * (pred - observed[:, :, None])
        resid_all = lax.all_gather(resid.astype(jnp.bfloat16), "band", axis=0, tiled=True)
        return (resid, adjoint_part(sensitivity, bundle_of, cellblock_of, resid_all, cell_blocks))

    probe1 = (state + 0.5 * prior_velocity).astype(jnp.bfloat16)
    res1, part1 = residual_pass(probe1)

    def summed_grad(part):
        return lax.psum(part, "shot")

    grad1 = summed_grad(part1)
    middle = state + 0.5 * (prior_velocity - 0.5 * grad1)
    probe2 = (middle + 0.5 * prior_velocity).astype(jnp.bfloat16)
    res2, part2 = residual_pass(probe2)
    grad2 = summed_grad(part2)
    new_state = state + 0.5 * (prior_velocity - 0.25 * (grad1 + grad2))
    return (new_state, res2)


def solution(mesh):
    in_specs = (
        P(("shot", "band"), None, None),
        P(("shot", "band")),
        P(("shot", "band")),
        P("band", None),
        P("band", None),
        P(("shot", "band"), None),
        P(("shot", "band"), None),
    )
    out_specs = (P("band", None), P(("shot", "band"), None, None))
    return jax.shard_map(
        per_device, mesh=mesh, in_specs=in_specs, out_specs=out_specs, check_vma=False
    )
```

profile of v0, /device:TPU:1, one launch (start us, length us, event | category | flops | bytes accessed | tf_op | source)
XLA Modules:
  0.0 844.5 jit_solution(9297075635177994917)
XLA Ops:
  9.7 2.2 gather_fusion
  11.8 5.2 convolution_bitcast_fusion.3
  17.0 5.6 copy.28
  24.2 13.5 %scatter_fusion = f32[32,128,128]{2,1,0:T(8,128)} fusion(f32[32,128,128]{2,1,0:T(8,128)} %broadcast.21.clone, s32[64]{0:T(128)S(1)} %copy-done.3, f32[64,128,128]{2,1,0:T(8,128)} %copy.28), kind=kCustom, calls=%fused_computation.4 | custom fusion | flops 1048576 | bytes 12583168 | tf_op jit(solution)/shard_map/scatter-add | solution.py:29
  37.8 214.6 %reduce-scatter.3.cloned.1.call-done = f32[1,128,128]{2,1,0:T(8,128)} async-done(((f32[32,128,128]{2,1,0:T(8,128)}), f32[1,128,128]{2,1,0:T(8,128)}) %reduce-scatter.3.cloned.1.call-update) | async-done | bytes 65552 | tf_op jit(solution)/shard_map/reduce_scatter | solution.py:30
  254.1 77.3 %all-gather.3.cloned.1.call-done = bf16[32,128,128]{2,1,0:T(8,128)(2,1)} async-done(((bf16[1,128,128]{2,1,0:T(8,128)(2,1)}), bf16[32,128,128]{2,1,0:T(8,128)(2,1)}) %all-gather.3.cloned.1.call-update) | async-done | bytes 1048592 | tf_op jit(solution)/shard_map/all_gather | solution.py:32
  331.4 3.4 gather_fusion.1
  334.7 4.4 convolution_bitcast_fusion.2
  339.1 5.6 copy.30
  344.8 8.8 %scatter_fusion.1 = f32[16,128,128]{2,1,0:T(8,128)S(1)} fusion(f32[16,128,128]{2,1,0:T(8,128)S(1)} %broadcast.20.clone, s32[64]{0:T(128)S(1)} %copy-done.6, f32[64,128,128]{2,1,0:T(8,128)} %copy.30), kind=kCustom, calls=%fused_computation.5 | custom fusion | flops 1048576 | bytes 12583168 | tf_op jit(solution)/shard_map/scatter-add | solution.py:17
  354.7 67.7 %all-reduce.3.cloned.1.call-done = f32[2048,128]{1,0:T(8,128)} async-done(((f32[2048,128]{1,0:T(8,128)}), f32[2048,128]{1,0:T(8,128)}) %all-reduce.3.cloned.1.call-update) | async-done | bytes 1048592 | tf_op jit(solution)/shard_map/psum | solution.py:39
  422.4 2.1 add_convert_fusion
  424.5 2.2 gather_fusion.2
  426.7 5.2 convolution_bitcast_fusion.1
  431.8 5.6 copy.32
  439.0 13.5 %scatter_fusion.2 = f32[32,128,128]{2,1,0:T(8,128)} fusion(f32[32,128,128]{2,1,0:T(8,128)} %broadcast.21, s32[64]{0:T(128)S(1)} %copy-done.3, f32[64,128,128]{2,1,0:T(8,128)} %copy.32), kind=kCustom, calls=%fused_computation.6 | custom fusion | flops 1048576 | bytes 12583168 | tf_op jit(solution)/shard_map/scatter-add | solution.py:29
  452.6 212.5 %reduce-scatter.5.cloned.1.call-done = f32[1,128,128]{2,1,0:T(8,128)} async-done(((f32[32,128,128]{2,1,0:T(8,128)}), f32[1,128,128]{2,1,0:T(8,128)}) %reduce-scatter.5.cloned.1.call-update) | async-done | bytes 65552 | tf_op jit(solution)/shard_map/reduce_scatter | solution.py:30
  667.0 76.4 %all-gather.5.cloned.1.call-done = bf16[32,128,128]{2,1,0:T(8,128)(2,1)} async-done(((bf16[1,128,128]{2,1,0:T(8,128)(2,1)}), bf16[32,128,128]{2,1,0:T(8,128)(2,1)}) %all-gather.5.cloned.1.call-update) | async-done | bytes 1048592 | tf_op jit(solution)/shard_map/all_gather | solution.py:32
  743.3 3.4 gather_fusion.3
  746.7 4.4 convolution_bitcast_fusion
  751.1 5.6 copy.34
  756.8 8.8 %scatter_fusion.3 = f32[16,128,128]{2,1,0:T(8,128)S(1)} fusion(f32[16,128,128]{2,1,0:T(8,128)S(1)} %broadcast.20, s32[64]{0:T(128)S(1)} %copy-done.6, f32[64,128,128]{2,1,0:T(8,128)} %copy.34), kind=kCustom, calls=%fused_computation.7 | custom fusion | flops 1048576 | bytes 12583168 | tf_op jit(solution)/shard_map/scatter-add | solution.py:17
  766.6 67.8 %all-reduce.5.cloned.1.call-done = f32[2048,128]{1,0:T(8,128)} async-done(((f32[2048,128]{1,0:T(8,128)}), f32[2048,128]{1,0:T(8,128)}) %all-reduce.5.cloned.1.call-update) | async-done | bytes 1048592 | tf_op jit(solution)/shard_map/psum | solution.py:39
  834.4 3.3 multiply_add_fusion
  (37 shorter events, 11.4 us)
Async XLA Ops:
  7.2 4.7 copy-start
  7.2 245.3 %reduce-scatter.3.cloned.1.call-start = ((), (), s32[]{:S(2)}) async-start(), calls=%async_computation.2 | async-start | bytes 2162688 | tf_op jit(solution)/shard_map/reduce_scatter | solution.py:30
  22.6 1.6 copy-start.3
  37.7 214.7 %copy-start.4 = (f32[1,128]{1,0:T(1,128)S(1)}, f32[1,128]{1,0:T(1,128)}, u32[]{:S(2)}) copy-start(f32[1,128]{1,0:T(1,128)} %param.12) | copy-start | bytes 1540
  37.7 214.7 %copy-start.5 = (f32[1,128]{1,0:T(1,128)S(1)}, f32[1,128]{1,0:T(1,128)}, u32[]{:S(2)}) copy-start(f32[1,128]{1,0:T(1,128)} %param.13) | copy-start | bytes 1540
  37.8 293.6 %all-gather.3.cloned.1.call-start = ((), (), s32[]{:S(2)}) async-start(), calls=%async_computation.3 | async-start | bytes 1081344 | tf_op jit(solution)/shard_map/all_gather | solution.py:32
  254.0 168.4 %all-reduce.3.cloned.1.call-start = ((), (), s32[]{:S(2)}) async-start(), calls=%async_computation.4 | async-start | bytes 2097152 | tf_op jit(solution)/shard_map/psum | solution.py:39
  339.1 5.7 copy-start.6
  353.6 1.0 copy-start.2
  354.6 310.5 %reduce-scatter.5.cloned.1.call-start = ((), (), s32[]{:S(2)}) async-start(), calls=%async_computation.5 | async-start | bytes 2162688 | tf_op jit(solution)/shard_map/reduce_scatter | solution.py:30
  452.6 290.8 %all-gather.5.cloned.1.call-start = ((), (), s32[]{:S(2)}) async-start(), calls=%async_computation.6 | async-start | bytes 1081344 | tf_op jit(solution)/shard_map/all_gather | solution.py:32
  666.7 167.6 %all-reduce.5.cloned.1.call-start = ((), (), s32[]{:S(2)}) async-start(), calls=%async_computation.7 | async-start | bytes 2097152 | tf_op jit(solution)/shard_map/psum | solution.py:39
  765.6 1.0 copy-start.1
Sparse Core Ops, SparseCore 0:
  37.9 214.5 reduce-scatter.2
  255.9 75.3 all-gather.2
  354.7 67.6 all-reduce.2
  452.7 212.3 reduce-scatter.4
  668.1 75.1 all-gather.4
  766.7 67.6 all-reduce.4
where the time goes:
time: 847 us; the launch traced here: 845 us
  waiting for transfers between devices  716 us (85%)
  other arithmetic  55.7 us (7%)
  local copies, waits for them, and re-layouts  38.7 us (5%)
  matrix products  19.1 us (2%)
  between operations  14.2 us (2%)
    reduce_scatter x2, waiting for transfers between devices, residual_pass(): lax.psum_scatter(partial_value, 'band', scatter_dimension=0, tiled=True)  427 us
    all_gather x2, waiting for transfers between devices, residual_pass(): lax.all_gather(resid.astype(jnp.bfloat16), 'band', axis=0, tiled=True)  154 us
    psum x2, waiting for transfers between devices, summed_grad(): return lax.psum(part, 'shot')  136 us
    scatter-add x2, other arithmetic, residual_pass(): partial_value = jax.ops.segment_sum(prod, bundle_of, num_segments=bundles)  27.1 us
    scatter-add x2, other arithmetic, adjoint_part(): jax.ops.segment_sum(contrib, cellblock_of, num_segments=cell_blocks)  17.6 us
  transfers between devices with their start and end apart: 6, of which 6 were waited for; matrix products, arithmetic and copies ran while one was open for 0% of the time, Pallas kernels for 0%

commit v1 on v0

v1 whole, which is shorter than its diff:
```python
import functools

import jax
import jax.numpy as jnp
from jax import lax
from jax.experimental import pallas as pl
from jax.experimental.pallas import tpu as pltpu
from jax.sharding import PartitionSpec as P

MESH = pl.DeviceIdType.MESH
BF16 = jnp.bfloat16
F32 = jnp.float32
I32 = jnp.int32
T = 128
NT_DIMS = (((1,), (1,)), ((), ()))
NN_DIMS = (((1,), (0,)), ((), ()))
UNROLL = 32
GROUPS = ((0, ((16, True), (48, False))), (64, ((16, True), (48, False))))
ORD_F, CEL_F, KEEP_F, LAST_F, ORD_A, BX_A, BZ_A, KEEP_A, LAST_A = range(9)


def band_grid(nband):
    nx = 4 if nband >= 16 else 2
    return nx, nband // nx


class Plan:
    def __init__(self, nshot, nband, nblk, ncell, groups):
        self.nx, self.nz = band_grid(nband)
        self.ns = nshot
        self.nblk, self.ncell, self.nband = nblk, ncell, nband
        self.cown = ncell // nshot
        self.groups = groups
        self.nsem = len(groups) * 2 * 2 + sum(8 * len(parts) for _, parts in groups)


def group_buffers(pn):
    bufs = {}
    for g, (row, parts) in enumerate(pn.groups):
        m = sum(rows for rows, _ in parts)
        bufs[f"pref{g}"] = ((pn.nblk + 1, m, T), F32)
        bufs[f"g1_{g}"] = ((pn.cown, m, T), F32)
        for p in range(2):
            bufs[f"Q{g}_{p}"] = ((pn.ncell, m, T), BF16)
            for d in "sr":
                bufs[f"y{d}{g}_{p}"] = ((pn.ns - 1, pn.cown, m, T), BF16)
            for u, (rows, zfirst) in enumerate(parts):
                first, second = (pn.nz, pn.nx) if zfirst else (pn.nx, pn.nz)
                k = f"{g}_{p}_{u}"
                bufs[f"acc{k}"] = ((second, rows, T), F32)
                bufs[f"R{k}"] = ((first, second, rows, T), BF16)
                for d in "sr":
                    bufs[f"a{d}{k}"] = ((first - 1, second, rows, T), BF16)
                    bufs[f"b{d}{k}"] = ((second - 1, rows, T), BF16)
    return bufs


def index_table(bun_ref, cel_ref, pad_ref, table_ref, pn):
    n = pn.nblk
    lane = lax.broadcasted_iota(I32, (T, T), 1)
    sub = lax.broadcasted_iota(I32, (T, T), 0)
    pad_ref[...] = jnp.full(pad_ref.shape, 127, I32)
    pad_ref[0:1, 0:n] = bun_ref[...].reshape(1, n)
    pad_ref[8:9, 0:n] = cel_ref[...].reshape(1, n)
    b = jnp.broadcast_to(pad_ref[0:1, :], (T, T))
    c = jnp.broadcast_to(pad_ref[8:9, :], (T, T))

    def ranked(key, other):
        key_t = key.T
        before = (key_t < key) | ((key_t == key) & (sub < lane))
        rank = jnp.sum(before.astype(I32), axis=0, keepdims=True)
        same = jnp.sum(((key_t == key) & (sub < lane)).astype(I32), axis=0, keepdims=True)
        keep = (same > 0).astype(I32)
        packed = rank * 65536 + keep * 16384 + other[0:1, :] * 128 + lane[0:1, :]
        packed = jnp.broadcast_to(packed, (T, T)).T
        mine = (packed // 65536) == lane
        row = jnp.sum(jnp.where(mine, packed % 65536, 0), axis=0, keepdims=True)
        upto = jnp.sum((key_t <= lane).astype(I32), axis=0, keepdims=True)
        held = jnp.sum((key_t == lane).astype(I32), axis=0, keepdims=True)
        last = jnp.where(held > 0, upto - 1, n)
        return row % 128, (row // 128) % 128, row // 16384, last

    order, other, keep, last = ranked(b, c)
    table_ref[ORD_F : ORD_F + 1, :] = order
    table_ref[CEL_F : CEL_F + 1, :] = other
    table_ref[KEEP_F : KEEP_F + 1, :] = keep
    table_ref[LAST_F : LAST_F + 1, :] = last
    order, other, keep, last = ranked(c, b)
    table_ref[ORD_A : ORD_A + 1, :] = order
    table_ref[BX_A : BX_A + 1, :] = other // pn.nz
    table_ref[BZ_A : BZ_A + 1, :] = other % pn.nz
    table_ref[KEEP_A : KEEP_A + 1, :] = keep
    table_ref[LAST_A : LAST_A + 1, :] = last


def kernel(pn, names, sens_hbm, bun_ref, cel_ref, state_hbm, prior_hbm, obs_ref, wgt_ref, new_ref, res_ref, *scratch):
    w = dict(zip(names, scratch))
    sens, state, prior = w["sens"], w["state"], w["prior"]
    tab, x1, res_t = w["tab"], w["x1"], w["res_t"]
    st_t, pr_t = w["st_t"], w["pr_t"]
    load_sem, send_sem, recv_sem = w["load_sem"], w["send_sem"], w["recv_sem"]
    nx, nz, ns, nblk, ncell, cown = pn.nx, pn.nz, pn.ns, pn.nblk, pn.ncell, pn.cown

    s, b = lax.axis_index("shot"), lax.axis_index("band")
    x, z = b // nz, b % nz
    size = {"x": nx, "s": ns, "z": nz}
    place = {"x": x, "s": s, "z": z}

    def at(axis, k):
        return (place[axis] + k) % size[axis]

    def device(axis, k):
        if axis == "x":
            return {"band": at("x", k) * nz + z}
        if axis == "z":
            return {"band": x * nz + at("z", k)}
        return {"shot": at("s", k)}

    def order(axis):
        n = size[axis]
        return sorted(range(1, n), key=lambda k: -min(k, n - k))

    load_state = pltpu.make_async_copy(state_hbm, state, load_sem.at[0])
    load_prior = pltpu.make_async_copy(prior_hbm, prior, load_sem.at[1])
    load_sens = pltpu.make_async_copy(sens_hbm, sens, load_sem.at[2])
    load_state.start()
    load_prior.start()
    load_sens.start()

    barrier = pltpu.get_barrier_semaphore()
    greet = [(axis, k) for axis in "xzs" for k in order(axis)]
    for axis, k in greet:
        pl.semaphore_signal(barrier, inc=1, device_id=device(axis, k), device_id_type=MESH)

    index_table(bun_ref, cel_ref, w["pad"], w["table"], pn)
    to_smem = pltpu.make_async_copy(w["table"], tab, load_sem.at[3])
    to_smem.start()

    load_state.wait()
    load_prior.wait()

    def probe_block(i, carry):
        x1[i] = (state[i] + 0.5 * prior[i]).astype(BF16).T
        return carry

    lax.fori_loop(0, ncell, probe_block, 0, unroll=4)
    for g in range(len(pn.groups)):
        w[f"pref{g}"][nblk] = jnp.zeros(w[f"pref{g}"].shape[1:], F32)
    to_smem.wait()
    load_sens.wait()

    counter = [0]
    sent = []
    first_send = [True]

    class Exchange:
        def __init__(self, axis, src_of, dst_of, send_all, recv_all):
            self.index = counter[0]
            counter[0] += 1
            self.recv_all = recv_all
            sent.append((self.index, send_all))
            if first_send[0]:
                first_send[0] = False
                pl.semaphore_wait(barrier, len(greet))
            for k in order(axis):
                pltpu.make_async_remote_copy(
                    src_ref=src_of(k), dst_ref=dst_of(k), send_sem=send_sem.at[self.index],
                    recv_sem=recv_sem.at[self.index], device_id=device(axis, k), device_id_type=MESH).start()

        def wait(self):
            pltpu.make_async_copy(self.recv_all, self.recv_all, recv_sem.at[self.index]).wait()

    def scatter(axis, fill, sbuf, rbuf):
        for k in order(axis):
            fill(at(axis, k), sbuf.at[k - 1])
        return Exchange(axis, lambda k: sbuf.at[k - 1], lambda k: rbuf.at[k - 1], sbuf, rbuf)

    def gather(axis, ref, chunk, n):
        mine = ref.at[pl.ds(place[axis] * chunk, chunk)]
        rest = ref.at[pl.ds(0, (n - 1) * chunk)]
        return Exchange(axis, lambda k: mine, lambda k: mine, rest, rest)

    def products(pref, m, order_row, keep_row, dims, field):
        def step(k, acc):
            prod = lax.dot_general(field(k), sens[tab[order_row, k]], dims, preferred_element_type=F32)
            acc = jnp.where(tab[keep_row, k] > 0, acc, 0.0) + prod
            pref[k] = acc
            return acc

        lax.fori_loop(0, nblk, step, jnp.zeros((m, T), F32), unroll=UNROLL)

    def group(g):
        row, parts = pn.groups[g]
        m = sum(rows for rows, _ in parts)
        starts = [sum(rows for rows, _ in parts[:u]) for u in range(len(parts))]
        pref, g1 = w[f"pref{g}"], w[f"g1_{g}"]
        span = slice(row, row + m)
        for p in range(2):
            Q = w[f"Q{g}_{p}"]
            ys, yr = w[f"ys{g}_{p}"], w[f"yr{g}_{p}"]

            def field_f(k):
                i = tab[CEL_F, k]
                return x1[i, span, :] if p == 0 else w[f"Q{g}_0"][i]

            products(pref, m, ORD_F, KEEP_F, NT_DIMS, field_f)

            def part(u):
                rows, zfirst = parts[u]
                key = f"{g}_{p}_{u}"
                asb, arb, bsb, brb = (w[q + key] for q in ("as", "ar", "bs", "br"))
                acc, R = w["acc" + key], w["R" + key]
                inner = slice(starts[u], starts[u] + rows)
                one, two = ("z", "x") if zfirst else ("x", "z")
                first, second = size[one], size[two]

                def term(d, c):
                    bundle = c * nz + d if zfirst else d * nz + c
                    return pref[tab[LAST_F, bundle], inner, :]

                def fill_one(d, ref):
                    for c in range(second):
                        ref[c] = term(d, c).astype(BF16)

                ex = scatter(one, fill_one, asb, arb)
                yield
                ex.wait()
                for c in range(second):
                    total = term(place[one], c)
                    for k in range(1, first):
                        total = total + arb[k - 1, c].astype(F32)
                    acc[c] = total

                def fill_two(d, ref):
                    ref[...] = acc[d].astype(BF16)

                ex = scatter(two, fill_two, bsb, brb)
                yield
                ex.wait()
                pred = acc[place[two]]
                for k in range(1, second):
                    pred = pred + brb[k - 1].astype(F32)
                r = wgt_ref[...] * (pred - obs_ref[...])
                if p == 1:
                    res_t[row + starts[u] : row + starts[u] + rows, :] = r
                R[place[one], place[two]] = r.astype(BF16)
                ex = gather(two, R.at[place[one]], 1, second)
                yield
                ex.wait()
                ex = gather(one, R, 1, first)
                yield
                ex.wait()

            running = [part(u) for u in range(len(parts))]
            for _ in range(4):
                for q in running:
                    next(q)
                yield
            for q in running:
                for _ in q:
                    pass

            def field_a(k):
                bx, bz = tab[BX_A, k], tab[BZ_A, k]
                pieces = []
                for u, (rows, zfirst) in enumerate(parts):
                    R = w[f"R{g}_{p}_{u}"]
                    pieces.append(R[bz, bx] if zfirst else R[bx, bz])
                return pieces[0] if len(pieces) == 1 else jnp.concatenate(pieces, axis=0)

            products(pref, m, ORD_A, KEEP_A, NN_DIMS, field_a)

            def grad_term(d, c):
                return pref[tab[LAST_A, d * cown + c]]

            def fill_grad(d, ref):
                for c in range(cown):
                    ref[c] = grad_term(d, c).astype(BF16)

            ex = scatter("s", fill_grad, ys, yr)
            if g == 0 and p == 0:
                for c in range(cown):
                    st_t[c] = state[s * cown + c].T
                    pr_t[c] = prior[s * cown + c].T
            yield
            ex.wait()
            for c in range(cown):
                grad = grad_term(s, c)
                for k in range(1, ns):
                    grad = grad + yr[k - 1, c].astype(F32)
                if p == 0:
                    g1[c] = grad
                    st, pr = st_t[c, span, :], pr_t[c, span, :]
                    middle = st + 0.5 * (pr - 0.5 * grad)
                    Q[s * cown + c] = (middle + 0.5 * pr).astype(BF16)
                else:
                    Q[s * cown + c] = (g1[c] + grad).astype(BF16)
            ex = gather("s", Q, cown, ns)
            yield
            ex.wait()

    live = [group(g) for g in range(len(pn.groups))]
    while live:
        for q in list(live):
            try:
                next(q)
            except StopIteration:
                live.remove(q)

    res_ref[0] = res_t[...].T

    def final_block(i, carry):
        pieces = [w[f"Q{g}_1"][i].astype(F32) for g in range(len(pn.groups))]
        total = jnp.concatenate(pieces, axis=0).T
        new_ref[i] = state[i] + 0.5 * (prior[i] - 0.25 * total)
        return carry

    lax.fori_loop(0, ncell, final_block, 0, unroll=4)
    for index, ref in sent:
        pltpu.make_async_copy(ref, ref, send_sem.at[index]).wait()


def per_device(pn, sensitivity, bundle_of, cellblock_of, state, prior_velocity, observed, pick_weight):
    ncell, nblk = pn.ncell, pn.nblk
    bufs = {
        "sens": ((nblk, T, T), BF16),
        "state": ((ncell, T, T), F32),
        "prior": ((ncell, T, T), F32),
        "x1": ((ncell, T, T), BF16),
        "res_t": ((T, T), F32),
        "st_t": ((pn.cown, T, T), F32),
        "pr_t": ((pn.cown, T, T), F32),
        "pad": ((16, T), I32),
        "table": ((16, T), I32),
    }
    bufs.update(group_buffers(pn))
    shapes = {k: pltpu.VMEM(*v) for k, v in bufs.items()}
    shapes["tab"] = pltpu.SMEM((16, T), I32)
    shapes["load_sem"] = pltpu.SemaphoreType.DMA((4,))
    shapes["send_sem"] = pltpu.SemaphoreType.DMA((pn.nsem,))
    shapes["recv_sem"] = pltpu.SemaphoreType.DMA((pn.nsem,))
    hbm = pl.BlockSpec(memory_space=pl.ANY)
    vmem = pl.BlockSpec(memory_space=pltpu.VMEM)
    new_state, res = pl.pallas_call(
        functools.partial(kernel, pn, list(shapes)),
        out_shape=(
            jax.ShapeDtypeStruct((ncell, T, T), F32),
            jax.ShapeDtypeStruct((1, T, T), F32),
        ),
        in_specs=[hbm, vmem, vmem, hbm, hbm, vmem, vmem],
        out_specs=(vmem, vmem),
        scratch_shapes=list(shapes.values()),
        compiler_params=pltpu.CompilerParams(
            collective_id=0, has_side_effects=True, vmem_limit_bytes=60 * 1024 * 1024),
        name="guided_update",
    )(sensitivity, bundle_of, cellblock_of, state.reshape(ncell, T, T), prior_velocity.reshape(ncell, T, T),
      observed, pick_weight)
    return new_state.reshape(ncell * T, T), res


def solution(mesh):
    nshot, nband = mesh.shape["shot"], mesh.shape["band"]
    in_specs = (
        P(("shot", "band"), None, None),
        P(("shot", "band")),
        P(("shot", "band")),
        P("band", None),
        P("band", None),
        P(("shot", "band"), None),
        P(("shot", "band"), None),
    )
    out_specs = (P("band", None), P(("shot", "band"), None, None))

    def body(sensitivity, bundle_of, cellblock_of, state, *rest):
        pn = Plan(nshot, nband, sensitivity.shape[0], state.shape[0] // T,
                  GROUPS)
        return per_device(pn, sensitivity, bundle_of, cellblock_of, state, *rest)

    return jax.shard_map(body, mesh=mesh, in_specs=in_specs, out_specs=out_specs, check_vma=False)
```

time: 847 us -> 94.8 us (0.11)
  waiting for transfers between devices: 716 us -> 0 us
  Pallas kernels: 0 us -> 91.1 us
  other arithmetic: 55.7 us -> 0 us
  local copies, waits for them, and re-layouts: 38.7 us -> 2.93 us
  matrix products: 19.1 us -> 0 us
  between operations: 14.2 us -> 0.65 us
    reduce_scatter x2 -> x0, waiting for transfers between devices: 427 us -> none  [residual_pass(): lax.psum_scatter(partial_value, 'band', scatter_dimension=0, tiled=True)]
    all_gather x2 -> x0, waiting for transfers between devices: 154 us -> none  [residual_pass(): lax.all_gather(resid.astype(jnp.bfloat16), 'band', axis=0, tiled=True)]
    psum x2 -> x0, waiting for transfers between devices: 136 us -> none  [summed_grad(): return lax.psum(part, 'shot')]
    pallas_call x0 -> x1, Pallas kernels: none -> 91.1 us  [per_device(): pl.pallas_call(functools.partial(kernel, pn, list(shapes)), out_shape=(ja...]
    scatter-add x4 -> x0, other arithmetic: 44.7 us -> none  [the longest x2 27.1 us: residual_pass(): partial_value = jax.ops.segment_sum(prod, bundle_of, num_segments=bundles)]
    dot_general x4 -> x0, local copies, waits for them, and re-layouts: 22.4 us -> none  [the longest x2 11.2 us: adjoint_part(): jnp.einsum('krc,kre->kce', sensitivity, rows, preferred_element_type=jnp....]
    dot_general x4 -> x0, matrix products: 19.1 us -> none  [the longest x2 10.4 us: block_products(): jnp.einsum('krc,kce->kre', sensitivity, columns, preferred_element_type=j...]
    gather x4 -> x0, local copies, waits for them, and re-layouts: 11 us -> none  [the longest x2 6.71 us: adjoint_part(): rows = resid_all[bundle_of]]
  transfers between devices with their start and end apart: 6 -> 0, of which waited for: 6 -> 0; matrix products, arithmetic and copies ran while one was open for 0% -> 0% of each run, Pallas kernels for 0% -> 0%
where the time goes in v1:
time: 94.8 us; the launch traced here: 94.7 us
  Pallas kernels  91.1 us (96%)
  local copies, waits for them, and re-layouts  2.93 us (3%)
    pallas_call x1, Pallas kernels, per_device(): pl.pallas_call(functools.partial(kernel, pn, list(shapes)), out_shape=(ja...  91.1 us
    unnamed x4, local copies, waits for them, and re-layouts  2.93 us

profile of v1, /device:TPU:1, one launch (start us, length us, event | category | flops | bytes accessed | tf_op | source)
XLA Modules:
  0.0 94.7 jit_solution(6590056685258967098)
XLA Ops:
  0.6 91.1 %guided_update.1 = (f32[16,128,128]{2,1,0:T(8,128)}, f32[1,128,128]{2,1,0:T(8,128)}) custom-call(bf16[64,128,128]{2,1,0:T(8,128)(2,1)} %sens_hbm.1, s32[64]{0:T(128)} %bun_ref.1, s32[64]{0:T(128)} %cel_ref.1, f32[16,128,128]{2,1,0:T(8,128)} %bitcast.4, f32[16,128,128]{2,1,0:T(8,128)} %bitcast.5, f32[1,128]{1,0:T(1,128)} %obs_ref.1, f32[1,128]{1,0:T(1,128)} %wgt_ref.1), custom_call_target="tpu_custom_call" | custom-call | tf_op jit(solution)/shard_map/guided_update/pallas_call | solution.py:344
  91.7 0.0 copy-start
  91.7 2.3 %copy.11 = f32[2048,128]{1,0:T(8,128)} copy(f32[2048,128]{1,0:T(8,128)} %bitcast.3) | data formatting | bytes 2097152
  94.0 0.0 copy-done
  94.0 0.6 copy.12
Async XLA Ops:
  91.7 2.3 %copy-start = (f32[1,128,128]{2,1,0:T(8,128)S(1)}, f32[1,128,128]{2,1,0:T(8,128)}, u32[]{:S(2)}) copy-start(f32[1,128,128]{2,1,0:T(8,128)} %get-tuple-element.9) | copy-start | bytes 196612

commit v2 on v1

v2 whole, which is shorter than its diff:
```python
import functools

import jax
import jax.numpy as jnp
from jax import lax
from jax.experimental import pallas as pl
from jax.experimental.pallas import tpu as pltpu
from jax.sharding import PartitionSpec as P

MESH = pl.DeviceIdType.MESH
BF16 = jnp.bfloat16
F32 = jnp.float32
I32 = jnp.int32
T = 128
NT_DIMS = (((1,), (1,)), ((), ()))
NN_DIMS = (((1,), (0,)), ((), ()))
UNROLL = 32
LAG = 0
VMEM_MB = 60
GROUPS = ((0, ((32, False),)), (32, ((16, True), (32, False))), (80, ((16, True), (32, False))))
ORD_F, CEL_F, KEEP_F, LAST_F, ORD_A, BX_A, BZ_A, KEEP_A, LAST_A, RX_A, RZ_A = range(11)


def band_grid(nband):
    nx = 4 if nband >= 16 else 2
    return nx, nband // nx


class Plan:
    def __init__(self, nshot, nband, nblk, ncell, groups):
        self.nx, self.nz = band_grid(nband)
        self.ny = nshot // 2
        self.nblk, self.ncell, self.nband = nblk, ncell, nband
        self.half = ncell // 2
        self.cown = ncell // nshot
        self.groups = groups
        self.nsem = len(groups) * 2 * 4 + sum(14 * len(parts) for _, parts in groups)


def spans(n):
    far = max(n // 2 - 1, 0)
    return [(0, n - far)] + ([(n - far, far)] if far else [])


def group_buffers(pn):
    bufs = {}
    for g, (row, parts) in enumerate(pn.groups):
        m = sum(rows for rows, _ in parts)
        bufs[f"pref{g}"] = ((pn.nblk + 1, m, T), F32)
        bufs[f"g1_{g}"] = ((pn.cown, m, T), F32)
        for p in range(2):
            bufs[f"Q{g}_{p}"] = ((pn.ncell, m, T), BF16)
            for d in "sr":
                bufs[f"c{d}{g}_{p}"] = ((pn.half, m, T), BF16)
                bufs[f"y{d}{g}_{p}"] = ((max(pn.ny - 1, 1), pn.cown, m, T), BF16)
            for u, (rows, zfirst) in enumerate(parts):
                first, second = (pn.nz, pn.nx) if zfirst else (pn.nx, pn.nz)
                k = f"{g}_{p}_{u}"
                bufs[f"own{k}"] = ((rows, T), F32)
                bufs[f"R{k}"] = ((first, second, rows, T), BF16)
                for d in "sr":
                    for q, (_, count) in enumerate(spans(second)):
                        bufs[f"a{d}{q}{k}"] = ((first - 1, count, rows, T), BF16)
                    bufs[f"b{d}{k}"] = ((second - 1, rows, T), BF16)
    return bufs


def index_table(bun_ref, cel_ref, pad_ref, table_ref, pn, x, z):
    n = pn.nblk
    lane = lax.broadcasted_iota(I32, (T, T), 1)
    sub = lax.broadcasted_iota(I32, (T, T), 0)
    pad_ref[...] = jnp.full(pad_ref.shape, 127, I32)
    pad_ref[0:1, 0:n] = bun_ref[...].reshape(1, n)
    pad_ref[8:9, 0:n] = cel_ref[...].reshape(1, n)
    b = jnp.broadcast_to(pad_ref[0:1, :], (T, T))
    c = jnp.broadcast_to(pad_ref[8:9, :], (T, T))

    def ranked(key, other):
        key_t = key.T
        before = (key_t < key) | ((key_t == key) & (sub < lane))
        rank = jnp.sum(before.astype(I32), axis=0, keepdims=True)
        same = jnp.sum(((key_t == key) & (sub < lane)).astype(I32), axis=0, keepdims=True)
        keep = (same > 0).astype(I32)
        packed = rank * 65536 + keep * 16384 + other[0:1, :] * 128 + lane[0:1, :]
        packed = jnp.broadcast_to(packed, (T, T)).T
        mine = (packed // 65536) == lane
        row = jnp.sum(jnp.where(mine, packed % 65536, 0), axis=0, keepdims=True)
        upto = jnp.sum((key_t <= lane).astype(I32), axis=0, keepdims=True)
        held = jnp.sum((key_t == lane).astype(I32), axis=0, keepdims=True)
        last = jnp.where(held > 0, upto - 1, n)
        return row % 128, (row // 128) % 128, row // 16384, last

    order, other, keep, last = ranked(b, c)
    table_ref[ORD_F : ORD_F + 1, :] = order
    table_ref[CEL_F : CEL_F + 1, :] = other
    table_ref[KEEP_F : KEEP_F + 1, :] = keep
    table_ref[LAST_F : LAST_F + 1, :] = last
    order, other, keep, last = ranked(c, b)
    table_ref[ORD_A : ORD_A + 1, :] = order
    table_ref[BX_A : BX_A + 1, :] = other // pn.nz
    table_ref[BZ_A : BZ_A + 1, :] = other % pn.nz
    table_ref[RX_A : RX_A + 1, :] = (other // pn.nz + (pn.nx + pn.nx // 4 - x)) % pn.nx
    table_ref[RZ_A : RZ_A + 1, :] = (other % pn.nz + (pn.nz + pn.nz // 4 - z)) % pn.nz
    table_ref[KEEP_A : KEEP_A + 1, :] = keep
    table_ref[LAST_A : LAST_A + 1, :] = last


def kernel(pn, names, sens_hbm, bun_hbm, cel_hbm, state_hbm, prior_hbm, obs_hbm, wgt_hbm, new_ref, res_ref, *scratch):
    w = dict(zip(names, scratch))
    sens, state, prior = w["sens"], w["state"], w["prior"]
    tab, x1, res_t = w["tab"], w["x1"], w["res_t"]
    st_t, pr_t = w["st_t"], w["pr_t"]
    load_sem, send_sem, recv_sem = w["load_sem"], w["send_sem"], w["recv_sem"]
    nx, nz, ny, nblk, ncell, half, cown = pn.nx, pn.nz, pn.ny, pn.nblk, pn.ncell, pn.half, pn.cown

    s, b = lax.axis_index("shot"), lax.axis_index("band")
    y, core = s // 2, s % 2
    x, z = b // nz, b % nz
    size = {"x": nx, "y": ny, "z": nz, "core": 2}
    place = {"x": x, "y": y, "z": z, "core": core}

    def at(axis, k):
        return (place[axis] + k) % size[axis]

    def device(axis, k):
        if axis == "x":
            return {"band": at("x", k) * nz + z}
        if axis == "z":
            return {"band": x * nz + at("z", k)}
        if axis == "y":
            return {"shot": at("y", k) * 2 + core}
        return {"shot": y * 2 + (1 - core)}

    def order(axis):
        n = size[axis]
        return sorted(range(1, n), key=lambda k: -min(k, n - k))

    small = []
    for q, (src, name) in enumerate(((bun_hbm, "bun"), (cel_hbm, "cel"), (obs_hbm, "obs"), (wgt_hbm, "wgt"))):
        small.append(pltpu.make_async_copy(src, w[name], load_sem.at[4 + q]))
        small[-1].start()
    obs_ref, wgt_ref = w["obs"], w["wgt"]
    load_state = pltpu.make_async_copy(state_hbm, state, load_sem.at[0])
    load_prior = pltpu.make_async_copy(prior_hbm, prior, load_sem.at[1])
    load_sens = pltpu.make_async_copy(sens_hbm, sens, load_sem.at[2])
    load_state.start()
    load_prior.start()
    load_sens.start()

    barrier = pltpu.get_barrier_semaphore()
    greet = [(axis, k) for axis in ("z", "x", "y", "core") for k in order(axis)]
    for axis, k in greet:
        pl.semaphore_signal(barrier, inc=1, device_id=device(axis, k), device_id_type=MESH)

    for load in small:
        load.wait()
    index_table(w["bun"], w["cel"], w["pad"], w["table"], pn, x, z)
    to_smem = pltpu.make_async_copy(w["table"], tab, load_sem.at[3])
    to_smem.start()

    load_state.wait()
    load_prior.wait()

    def probe_block(i, carry):
        x1[i] = (state[i] + 0.5 * prior[i]).astype(BF16).T
        return carry

    lax.fori_loop(0, ncell, probe_block, 0, unroll=4)
    for g in range(len(pn.groups)):
        w[f"pref{g}"][nblk] = jnp.zeros(w[f"pref{g}"].shape[1:], F32)
    to_smem.wait()
    load_sens.wait()

    counter = [0]
    sent = []
    first_send = [True]

    class Exchange:
        def __init__(self, axis, sent_all, came_all):
            self.axis, self.came_all = axis, came_all
            self.index = counter[0]
            counter[0] += 1
            sent.append((self.index, sent_all))
            if first_send[0]:
                first_send[0] = False
                pl.semaphore_wait(barrier, len(greet))

        def send(self, k, src, dst):
            pltpu.make_async_remote_copy(
                src_ref=src, dst_ref=dst, send_sem=send_sem.at[self.index], recv_sem=recv_sem.at[self.index],
                device_id=device(self.axis, k), device_id_type=MESH).start()

        def wait(self):
            pltpu.make_async_copy(self.came_all, self.came_all, recv_sem.at[self.index]).wait()

    def products(pref, m, order_row, keep_row, dims, field):
        def step(k, acc):
            prod = lax.dot_general(field(k), sens[tab[order_row, k]], dims, preferred_element_type=F32)
            acc = jnp.where(tab[keep_row, k] > 0, acc, 0.0) + prod
            pref[k] = acc
            return acc

        lax.fori_loop(0, nblk, step, jnp.zeros((m, T), F32), unroll=UNROLL)

    def group(g):
        row, parts = pn.groups[g]
        m = sum(rows for rows, _ in parts)
        starts = [sum(rows for rows, _ in parts[:u]) for u in range(len(parts))]
        pref, g1 = w[f"pref{g}"], w[f"g1_{g}"]
        span = slice(row, row + m)
        for p in range(2):
            Q = w[f"Q{g}_{p}"]
            ys, yr = w[f"ys{g}_{p}"], w[f"yr{g}_{p}"]

            def field_f(k):
                i = tab[CEL_F, k]
                return x1[i, span, :] if p == 0 else w[f"Q{g}_0"][i]

            products(pref, m, ORD_F, KEEP_F, NT_DIMS, field_f)

            def part(u):
                rows, zfirst = parts[u]
                key = f"{g}_{p}_{u}"
                bsb, brb, own, R = (w[q + key] for q in ("bs", "br", "own", "R"))
                inner = slice(starts[u], starts[u] + rows)
                one, two = ("z", "x") if zfirst else ("x", "z")
                first, second = size[one], size[two]
                back = second // 4
                mine = place[one]

                def term(d, c):
                    bundle = c * nz + d if zfirst else d * nz + c
                    return pref[tab[LAST_F, bundle], inner, :]

                opened = []
                for q, (low, count) in reversed(list(enumerate(spans(second)))):
                    asb, arb = w[f"as{q}" + key], w[f"ar{q}" + key]
                    ex = Exchange(one, asb, arb)
                    for k in order(one):
                        for j in range(count):
                            asb[k - 1, j] = term(at(one, k), at(two, low + j - back + second)).astype(BF16)
                        ex.send(k, asb.at[k - 1], arb.at[k - 1])
                    opened.append((ex, arb, low, count))
                yield
                across = Exchange(two, bsb, brb)
                for ex, arb, low, count in opened:
                    ex.wait()
                    for j in range(count):
                        k2 = (low + j - back) % second
                        total = term(mine, at(two, k2))
                        for k in range(1, first):
                            total = total + arb[k - 1, j].astype(F32)
                        if k2 == 0:
                            own[...] = total
                        else:
                            bsb[k2 - 1] = total.astype(BF16)
                            across.send(k2, bsb.at[k2 - 1], brb.at[k2 - 1])
                yield
                across.wait()
                pred = own[...]
                for k in range(1, second):
                    pred = pred + brb[k - 1].astype(F32)
                r = wgt_ref[...] * (pred - obs_ref[...])
                if p == 1:
                    res_t[row + starts[u] : row + starts[u] + rows, :] = r
                R[mine, back] = r.astype(BF16)
                opened = []
                for low, count in reversed(spans(second)):
                    steps = [(low + j - back) % second for j in range(count)]
                    steps = [k for k in steps if k]
                    every = R.at[0, pl.ds(0, len(steps))]
                    ex = Exchange(two, every, every)
                    for k in steps:
                        ex.send(k, R.at[mine, back], R.at[mine, (back - k) % second])
                    opened.append((ex, low, count))
                yield
                across = []
                for ex, low, count in reversed(opened):
                    ex.wait()
                    every = R.at[pl.ds(0, first - 1), pl.ds(0, count)]
                    out = Exchange(one, every, every)
                    ref = R.at[mine, pl.ds(low, count)]
                    for k in order(one):
                        out.send(k, ref, ref)
                    across.append(out)
                yield
                for out in across:
                    out.wait()

            running = [part(u) for u in range(len(parts))]
            for _ in range(4):
                for q in running:
                    next(q)
                yield
            for q in running:
                for _ in q:
                    pass

            def field_a(k):
                pieces = []
                for u, (rows, zfirst) in enumerate(parts):
                    R = w[f"R{g}_{p}_{u}"]
                    pieces.append(R[tab[BZ_A, k], tab[RX_A, k]] if zfirst else R[tab[BX_A, k], tab[RZ_A, k]])
                return pieces[0] if len(pieces) == 1 else jnp.concatenate(pieces, axis=0)

            products(pref, m, ORD_A, KEEP_A, NN_DIMS, field_a)

            cs, cr = w[f"cs{g}_{p}"], w[f"cr{g}_{p}"]
            for i in range(half):
                cs[i] = pref[tab[LAST_A, (1 - core) * half + i]].astype(BF16)
            ex = Exchange("core", cs, cr)
            ex.send(1, cs, cr)
            if g == 0 and p == 0:
                for c in range(cown):
                    st_t[c] = state[core * half + y * cown + c].T
                    pr_t[c] = prior[core * half + y * cown + c].T
            yield
            ex.wait()

            def grad_term(d, c):
                i = d * cown + c
                return pref[tab[LAST_A, core * half + i]] + cr[i].astype(F32)

            if ny > 1:
                ex = Exchange("y", ys, yr)
                for k in order("y"):
                    for c in range(cown):
                        ys[k - 1, c] = grad_term(at("y", k), c).astype(BF16)
                    ex.send(k, ys.at[k - 1], yr.at[k - 1])
                yield
                ex.wait()
            base = core * half + y * cown
            for c in range(cown):
                grad = grad_term(y, c)
                for k in range(1, ny):
                    grad = grad + yr[k - 1, c].astype(F32)
                if p == 0:
                    g1[c] = grad
                    st, pr = st_t[c, span, :], pr_t[c, span, :]
                    middle = st + 0.5 * (pr - 0.5 * grad)
                    Q[base + c] = (middle + 0.5 * pr).astype(BF16)
                else:
                    Q[base + c] = (g1[c] + grad).astype(BF16)
            if ny > 1:
                rest = Q.at[pl.ds(0, (ny - 1) * cown)]
                ref = Q.at[pl.ds(base, cown)]
                ex = Exchange("y", rest, rest)
                for k in order("y"):
                    ex.send(k, ref, ref)
                yield
                ex.wait()
            ref = Q.at[pl.ds(core * half, half)]
            ex = Exchange("core", ref, ref)
            ex.send(1, ref, ref)
            if p == 1:
                last.append(ex)
                return
            yield
            ex.wait()

    last = []
    live = [(g * LAG, group(g)) for g in range(len(pn.groups))]
    tick = 0
    while live:
        for start, q in list(live):
            if tick >= start and next(q, "end") == "end":
                live.remove((start, q))
        tick += 1

    res_ref[0] = res_t[...].T

    def final_block(i, start):
        pieces = [w[f"Q{g}_1"][start + i].astype(F32) for g in range(len(pn.groups))]
        total = jnp.concatenate(pieces, axis=0).T
        new_ref[start + i] = state[start + i] + 0.5 * (prior[start + i] - 0.25 * total)
        return start

    lax.fori_loop(0, half, final_block, core * half, unroll=4)
    for ex in last:
        ex.wait()
    lax.fori_loop(0, half, final_block, (1 - core) * half, unroll=4)
    for index, ref in sent:
        pltpu.make_async_copy(ref, ref, send_sem.at[index]).wait()


def per_device(pn, sensitivity, bundle_of, cellblock_of, state, prior_velocity, observed, pick_weight):
    ncell, nblk = pn.ncell, pn.nblk
    bufs = {
        "sens": ((nblk, T, T), BF16),
        "state": ((ncell, T, T), F32),
        "prior": ((ncell, T, T), F32),
        "x1": ((ncell, T, T), BF16),
        "res_t": ((T, T), F32),
        "st_t": ((pn.cown, T, T), F32),
        "pr_t": ((pn.cown, T, T), F32),
        "bun": ((nblk,), I32),
        "cel": ((nblk,), I32),
        "obs": ((1, T), F32),
        "wgt": ((1, T), F32),
        "pad": ((16, T), I32),
        "table": ((16, T), I32),
    }
    bufs.update(group_buffers(pn))
    shapes = {k: pltpu.VMEM(*v) for k, v in bufs.items()}
    shapes["tab"] = pltpu.SMEM((16, T), I32)
    shapes["load_sem"] = pltpu.SemaphoreType.DMA((8,))
    shapes["send_sem"] = pltpu.SemaphoreType.DMA((pn.nsem,))
    shapes["recv_sem"] = pltpu.SemaphoreType.DMA((pn.nsem,))
    hbm = pl.BlockSpec(memory_space=pltpu.HBM)
    vmem = pl.BlockSpec(memory_space=pltpu.VMEM)
    new_state, res = pl.pallas_call(
        functools.partial(kernel, pn, list(shapes)),
        out_shape=(
            jax.ShapeDtypeStruct((ncell, T, T), F32),
            jax.ShapeDtypeStruct((1, T, T), F32),
        ),
        in_specs=[hbm] * 7,
        out_specs=(vmem, vmem),
        scratch_shapes=list(shapes.values()),
        compiler_params=pltpu.CompilerParams(
            collective_id=0, has_side_effects=True, vmem_limit_bytes=VMEM_MB * 1024 * 1024),
        name="guided_update",
    )(sensitivity, bundle_of, cellblock_of, state.reshape(ncell, T, T), prior_velocity.reshape(ncell, T, T),
      observed, pick_weight)
    return new_state.reshape(ncell * T, T), res


def solution(mesh):
    nshot, nband = mesh.shape["shot"], mesh.shape["band"]
    in_specs = (
        P(("shot", "band"), None, None),
        P(("shot", "band")),
        P(("shot", "band")),
        P("band", None),
        P("band", None),
        P(("shot", "band"), None),
        P(("shot", "band"), None),
    )
    out_specs = (P("band", None), P(("shot", "band"), None, None))

    def body(sensitivity, bundle_of, cellblock_of, state, *rest):
        pn = Plan(nshot, nband, sensitivity.shape[0], state.shape[0] // T,
                  GROUPS)
        return per_device(pn, sensitivity, bundle_of, cellblock_of, state, *rest)

    return jax.shard_map(body, mesh=mesh, in_specs=in_specs, out_specs=out_specs, check_vma=False)
```

time: 94.8 us -> 91.4 us (0.964)
  Pallas kernels: 91.1 us -> 87.7 us
    pallas_call x1, Pallas kernels: 91.1 us -> 87.7 us  [per_device(): pl.pallas_call(functools.partial(kernel, pn, list(shapes)), out_shape=(ja...]
where the time goes in v2:
time: 91.4 us; the launch traced here: 91.2 us
  Pallas kernels  87.7 us (96%)
  local copies, waits for them, and re-layouts  2.93 us (3%)
    pallas_call x1, Pallas kernels, per_device(): pl.pallas_call(functools.partial(kernel, pn, list(shapes)), out_shape=(ja...  87.7 us
    unnamed x4, local copies, waits for them, and re-layouts  2.93 us

profile of v2, /device:TPU:1, one launch (start us, length us, event | category | flops | bytes accessed | tf_op | source)
XLA Modules:
  0.0 91.2 jit_solution(11819983882841945606)
XLA Ops:
  0.6 87.7 %guided_update.1 = (f32[16,128,128]{2,1,0:T(8,128)}, f32[1,128,128]{2,1,0:T(8,128)}) custom-call(bf16[64,128,128]{2,1,0:T(8,128)(2,1)} %sens_hbm.1, s32[64]{0:T(128)} %bun_hbm.1, s32[64]{0:T(128)} %cel_hbm.1, f32[16,128,128]{2,1,0:T(8,128)} %bitcast.4, f32[16,128,128]{2,1,0:T(8,128)} %bitcast.5, f32[1,128]{1,0:T(1,128)} %obs_hbm.1, f32[1,128]{1,0:T(1,128)} %wgt_hbm.1), custom_call_target="tpu_custom_call" | custom-call | tf_op jit(solution)/shard_map/guided_update/pallas_call | solution.py:411
  88.3 0.0 copy-start
  88.3 2.3 %copy.11 = f32[2048,128]{1,0:T(8,128)} copy(f32[2048,128]{1,0:T(8,128)} %bitcast.3) | data formatting | bytes 2097152
  90.6 0.0 copy-done
  90.6 0.6 copy.12
Async XLA Ops:
  88.3 2.3 %copy-start = (f32[1,128,128]{2,1,0:T(8,128)S(1)}, f32[1,128,128]{2,1,0:T(8,128)}, u32[]{:S(2)}) copy-start(f32[1,128,128]{2,1,0:T(8,128)} %get-tuple-element.9) | copy-start | bytes 196612

commit v3 on v2

--- a/solution.py
+++ b/solution.py
@@ -14,7 +14,7 @@
 T = 128
 NT_DIMS = (((1,), (1,)), ((), ()))
 NN_DIMS = (((1,), (0,)), ((), ()))
-UNROLL = 32
+UNROLL = 64
 LAG = 0
 VMEM_MB = 60
 GROUPS = ((0, ((32, False),)), (32, ((16, True), (32, False))), (80, ((16, True), (32, False))))
@@ -172,22 +172,20 @@
     load_sens.wait()
 
     counter = [0]
-    sent = []
     first_send = [True]
 
     class Exchange:
-        def __init__(self, axis, sent_all, came_all):
-            self.axis, self.came_all = axis, came_all
+        def __init__(self, axis, out, came_all):
+            self.axis, self.out, self.came_all = axis, out, came_all
             self.index = counter[0]
             counter[0] += 1
-            sent.append((self.index, sent_all))
             if first_send[0]:
                 first_send[0] = False
                 pl.semaphore_wait(barrier, len(greet))
 
         def send(self, k, src, dst):
             pltpu.make_async_remote_copy(
-                src_ref=src, dst_ref=dst, send_sem=send_sem.at[self.index], recv_sem=recv_sem.at[self.index],
+                src_ref=src, dst_ref=dst, send_sem=send_sem.at[self.out], recv_sem=recv_sem.at[self.index],
                 device_id=device(self.axis, k), device_id_type=MESH).start()
 
         def wait(self):
@@ -209,6 +207,7 @@
         pref, g1 = w[f"pref{g}"], w[f"g1_{g}"]
         span = slice(row, row + m)
         for p in range(2):
+            out = 2 * g + p
             Q = w[f"Q{g}_{p}"]
             ys, yr = w[f"ys{g}_{p}"], w[f"yr{g}_{p}"]
 
@@ -235,14 +234,14 @@
                 opened = []
                 for q, (low, count) in reversed(list(enumerate(spans(second)))):
                     asb, arb = w[f"as{q}" + key], w[f"ar{q}" + key]
-                    ex = Exchange(one, asb, arb)
+                    ex = Exchange(one, out, arb)
                     for k in order(one):
                         for j in range(count):
                             asb[k - 1, j] = term(at(one, k), at(two, low + j - back + second)).astype(BF16)
                         ex.send(k, asb.at[k - 1], arb.at[k - 1])
                     opened.append((ex, arb, low, count))
                 yield
-                across = Exchange(two, bsb, brb)
+                across = Exchange(two, out, brb)
                 for ex, arb, low, count in opened:
                     ex.wait()
                     for j in range(count):
@@ -269,7 +268,7 @@
                     steps = [(low + j - back) % second for j in range(count)]
                     steps = [k for k in steps if k]
                     every = R.at[0, pl.ds(0, len(steps))]
-                    ex = Exchange(two, every, every)
+                    ex = Exchange(two, out, every)
                     for k in steps:
                         ex.send(k, R.at[mine, back], R.at[mine, (back - k) % second])
                     opened.append((ex, low, count))
@@ -278,14 +277,14 @@
                 for ex, low, count in reversed(opened):
                     ex.wait()
                     every = R.at[pl.ds(0, first - 1), pl.ds(0, count)]
-                    out = Exchange(one, every, every)
+                    spread = Exchange(one, out, every)
                     ref = R.at[mine, pl.ds(low, count)]
                     for k in order(one):
-                        out.send(k, ref, ref)
-                    across.append(out)
-                yield
-                for out in across:
-                    out.wait()
+                        spread.send(k, ref, ref)
+                    across.append(spread)
+                yield
+                for ex in across:
+                    ex.wait()
 
             running = [part(u) for u in range(len(parts))]
             for _ in range(4):
@@ -308,7 +307,7 @@
             cs, cr = w[f"cs{g}_{p}"], w[f"cr{g}_{p}"]
             for i in range(half):
                 cs[i] = pref[tab[LAST_A, (1 - core) * half + i]].astype(BF16)
-            ex = Exchange("core", cs, cr)
+            ex = Exchange("core", out, cr)
             ex.send(1, cs, cr)
             if g == 0 and p == 0:
                 for c in range(cown):
@@ -322,7 +321,7 @@
                 return pref[tab[LAST_A, core * half + i]] + cr[i].astype(F32)
 
             if ny > 1:
-                ex = Exchange("y", ys, yr)
+                ex = Exchange("y", out, yr)
                 for k in order("y"):
                     for c in range(cown):
                         ys[k - 1, c] = grad_term(at("y", k), c).astype(BF16)
@@ -344,13 +343,13 @@
             if ny > 1:
                 rest = Q.at[pl.ds(0, (ny - 1) * cown)]
                 ref = Q.at[pl.ds(base, cown)]
-                ex = Exchange("y", rest, rest)
+                ex = Exchange("y", out, rest)
                 for k in order("y"):
                     ex.send(k, ref, ref)
                 yield
                 ex.wait()
             ref = Q.at[pl.ds(core * half, half)]
-            ex = Exchange("core", ref, ref)
+            ex = Exchange("core", out, ref)
             ex.send(1, ref, ref)
             if p == 1:
                 last.append(ex)
@@ -379,8 +378,11 @@
     for ex in last:
         ex.wait()
     lax.fori_loop(0, half, final_block, (1 - core) * half, unroll=4)
-    for index, ref in sent:
-        pltpu.make_async_copy(ref, ref, send_sem.at[index]).wait()
+    units = pn.nband - 1 + half + (ny - 1) * cown
+    for g in range(len(pn.groups)):
+        for p in range(2):
+            every = w[f"pref{g}"].at[pl.ds(0, units)]
+            pltpu.make_async_copy(every, every, send_sem.at[2 * g + p]).wait()
 
 
 def per_device(pn, sensitivity, bundle_of, cellblock_of, state, prior_velocity, observed, pick_weight):
@@ -404,7 +406,7 @@
     shapes = {k: pltpu.VMEM(*v) for k, v in bufs.items()}
     shapes["tab"] = pltpu.SMEM((16, T), I32)
     shapes["load_sem"] = pltpu.SemaphoreType.DMA((8,))
-    shapes["send_sem"] = pltpu.SemaphoreType.DMA((pn.nsem,))
+    shapes["send_sem"] = pltpu.SemaphoreType.DMA((2 * len(pn.groups),))
     shapes["recv_sem"] = pltpu.SemaphoreType.DMA((pn.nsem,))
     hbm = pl.BlockSpec(memory_space=pltpu.HBM)
     vmem = pl.BlockSpec(memory_space=pltpu.VMEM)

time: 91.4 us -> 89.6 us (0.980)
  Pallas kernels: 87.7 us -> 85.9 us
    pallas_call x1, Pallas kernels: 87.7 us -> 85.9 us  [per_device(): pl.pallas_call(functools.partial(kernel, pn, list(shapes)), out_shape=(ja...]
where the time goes in v3:
time: 89.6 us; the launch traced here: 89.5 us
  Pallas kernels  85.9 us (96%)
  local copies, waits for them, and re-layouts  2.93 us (3%)
    pallas_call x1, Pallas kernels, per_device(): pl.pallas_call(functools.partial(kernel, pn, list(shapes)), out_shape=(ja...  85.9 us
    unnamed x4, local copies, waits for them, and re-layouts  2.93 us

profile of v3, /device:TPU:1, one launch (start us, length us, event | category | flops | bytes accessed | tf_op | source)
XLA Modules:
  0.0 89.5 jit_solution(12182266127552531637)
XLA Ops:
  0.6 85.9 %guided_update.1 = (f32[16,128,128]{2,1,0:T(8,128)}, f32[1,128,128]{2,1,0:T(8,128)}) custom-call(bf16[64,128,128]{2,1,0:T(8,128)(2,1)} %sens_hbm.1, s32[64]{0:T(128)} %bun_hbm.1, s32[64]{0:T(128)} %cel_hbm.1, f32[16,128,128]{2,1,0:T(8,128)} %bitcast.4, f32[16,128,128]{2,1,0:T(8,128)} %bitcast.5, f32[1,128]{1,0:T(1,128)} %obs_hbm.1, f32[1,128]{1,0:T(1,128)} %wgt_hbm.1), custom_call_target="tpu_custom_call" | custom-call | tf_op jit(solution)/shard_map/guided_update/pallas_call | solution.py:413
  86.6 0.0 copy-start
  86.6 2.3 %copy.11 = f32[2048,128]{1,0:T(8,128)} copy(f32[2048,128]{1,0:T(8,128)} %bitcast.3) | data formatting | bytes 2097152
  88.9 0.0 copy-done
  88.9 0.6 copy.12
Async XLA Ops:
  86.6 2.3 %copy-start = (f32[1,128,128]{2,1,0:T(8,128)S(1)}, f32[1,128,128]{2,1,0:T(8,128)}, u32[]{:S(2)}) copy-start(f32[1,128,128]{2,1,0:T(8,128)} %get-tuple-element.9) | copy-start | bytes 196612

commit v4 on v3

--- a/solution.py
+++ b/solution.py
@@ -177,7 +177,7 @@
     class Exchange:
         def __init__(self, axis, out, came_all):
             self.axis, self.out, self.came_all = axis, out, came_all
-            self.index = counter[0]
+            self.index = counter[0] % (pn.nsem // 2)
             counter[0] += 1
             if first_send[0]:
                 first_send[0] = False
@@ -407,7 +407,7 @@
     shapes["tab"] = pltpu.SMEM((16, T), I32)
     shapes["load_sem"] = pltpu.SemaphoreType.DMA((8,))
     shapes["send_sem"] = pltpu.SemaphoreType.DMA((2 * len(pn.groups),))
-    shapes["recv_sem"] = pltpu.SemaphoreType.DMA((pn.nsem,))
+    shapes["recv_sem"] = pltpu.SemaphoreType.DMA((pn.nsem // 2,))
     hbm = pl.BlockSpec(memory_space=pltpu.HBM)
     vmem = pl.BlockSpec(memory_space=pltpu.VMEM)
     new_state, res = pl.pallas_call(

time: 89.6 us -> 88.9 us (level)
  no operation moved by 1% of the time
where the time goes in v4:
time: 88.9 us; the launch traced here: 88.8 us
  Pallas kernels  85.2 us (96%)
  local copies, waits for them, and re-layouts  2.93 us (3%)
    pallas_call x1, Pallas kernels, per_device(): pl.pallas_call(functools.partial(kernel, pn, list(shapes)), out_shape=(ja...  85.2 us
    unnamed x4, local copies, waits for them, and re-layouts  2.93 us

profile of v4, /device:TPU:1, one launch (start us, length us, event | category | flops | bytes accessed | tf_op | source)
XLA Modules:
  0.0 88.8 jit_solution(7176551445875425908)
XLA Ops:
  0.6 85.2 %guided_update.1 = (f32[16,128,128]{2,1,0:T(8,128)}, f32[1,128,128]{2,1,0:T(8,128)}) custom-call(bf16[64,128,128]{2,1,0:T(8,128)(2,1)} %sens_hbm.1, s32[64]{0:T(128)} %bun_hbm.1, s32[64]{0:T(128)} %cel_hbm.1, f32[16,128,128]{2,1,0:T(8,128)} %bitcast.4, f32[16,128,128]{2,1,0:T(8,128)} %bitcast.5, f32[1,128]{1,0:T(1,128)} %obs_hbm.1, f32[1,128]{1,0:T(1,128)} %wgt_hbm.1), custom_call_target="tpu_custom_call" | custom-call | tf_op jit(solution)/shard_map/guided_update/pallas_call | solution.py:413
  85.8 0.0 copy-start
  85.8 2.3 %copy.11 = f32[2048,128]{1,0:T(8,128)} copy(f32[2048,128]{1,0:T(8,128)} %bitcast.3) | data formatting | bytes 2097152
  88.1 0.0 copy-done
  88.1 0.6 copy.12
Async XLA Ops:
  85.8 2.3 %copy-start = (f32[1,128,128]{2,1,0:T(8,128)S(1)}, f32[1,128,128]{2,1,0:T(8,128)}, u32[]{:S(2)}) copy-start(f32[1,128,128]{2,1,0:T(8,128)} %get-tuple-element.9) | copy-start | bytes 196612
